TPU v7x, 512 devices: a whole 4x8x8 slice. The times are simulated.
512 devices in a mesh: ctx: 64 (over z, y), head: 8 (over x, core).
Axes of the slice: x: 4, y: 8, z: 8, core: 2. Of those that a mesh axis runs over, the one named last changes fastest.
Arguments:
- queries: bfloat16 [512, 8192], P('ctx', 'head'), may hold values from -6 to 6
- cache_keys: bfloat16 [65536, 8, 128], P('ctx', 'head'), may hold values from -6 to 6
- cache_values: bfloat16 [65536, 8, 128], P('ctx', 'head'), may hold values from -6 to 6
- vertical_blocks: int32 [64, 8], P('head'), may hold values from 0 to 511, as said below
- slash_offsets: int32 [64, 48], P('head'), may hold values from 0 to 511, as said below
- out_weight: bfloat16 [8192, 8192], P('head', 'ctx'), may hold values from -0.0625 to 0.0625
Outputs:
- projected: bfloat16 [512, 8192], P('head', 'ctx')
Inputs may be any that keep to these rules, and one draw needn't show every extreme that they name: `vertical_blocks`: every head's list holds block 0; entries may repeat, and a block counts once however often it is named. `slash_offsets`: every head's list holds offset 0; entries may repeat, and a block counts once however often it is reached.
All inputs are finite; a program needn't handle non-finite values.
Results may differ from a plain program's by a relative error of at most 0.007.
Values may be sent and summed in bfloat16 or wider, within the bound.
A program may use at most 64 MiB of HBM per device.

v0:
```python
from functools import partial
import jax
import jax.numpy as jnp
from jax import lax
from jax.sharding import PartitionSpec as P

BLOCK = 128
NEG_FILL = -1e30


def block_terms(q_four, key_block, value_block, allowed_mask, score_scale):
    kv_local = q_four.shape[1]
    group_size = q_four.shape[2]
    scores = (
        jnp.einsum("qgjd,kgd->qgjk", q_four, key_block, preferred_element_type=jnp.float32)
        * score_scale
    )
    scores = scores.reshape(scores.shape[0], kv_local * group_size, scores.shape[3])
    masked = jnp.where(allowed_mask, scores, NEG_FILL)
    block_peak = jnp.max(masked, axis=-1)
    safe_peak = jnp.where(block_peak > 0.5 * NEG_FILL, block_peak, 0.0)
    weights = jnp.where(allowed_mask, jnp.exp(scores - safe_peak[..., None]), 0.0).astype(
        jnp.bfloat16
    )
    block_total = jnp.sum(weights.astype(jnp.float32), axis=-1)
    weights_four = weights.reshape(weights.shape[0], kv_local, group_size, weights.shape[2])
    block_out = jnp.einsum(
        "qgjk,kgd->qgjd", weights_four, value_block, preferred_element_type=jnp.float32
    )
    return (
        block_peak,
        block_total,
        block_out.reshape(block_out.shape[0], kv_local * group_size, block_out.shape[3]),
    )


def body(queries, cache_keys, cache_values, vertical_blocks, slash_offsets, out_weight):
    ctx_count = lax.axis_size("ctx")
    ctx_place = lax.axis_index("ctx")
    q_whole = lax.all_gather(queries, "ctx", axis=0, tiled=True)
    q_total = q_whole.shape[0]
    local_len, kv_local, head_width = cache_keys.shape
    heads_local = vertical_blocks.shape[0]
    group_size = heads_local // kv_local
    local_blocks = local_len // BLOCK
    q_blocks = q_total // BLOCK
    all_blocks = local_blocks * ctx_count
    score_scale = float(head_width) ** (-0.5)
    q_four = q_whole.reshape(q_total, kv_local, group_size, head_width)
    block_ids = ctx_place * local_blocks + jnp.arange(local_blocks, dtype=jnp.int32)
    query_blocks = all_blocks - q_blocks + jnp.arange(q_blocks, dtype=jnp.int32)
    vertical_hit = jnp.any(vertical_blocks[:, :, None] == block_ids[None, None, :], axis=1)
    offsets = query_blocks[:, None] - block_ids[None, :]
    slash_hit = jnp.any(slash_offsets[:, None, None, :] == offsets[None, :, :, None], axis=3)
    chosen = jnp.transpose(vertical_hit[:, None, :] | slash_hit, (1, 0, 2))
    first_query = all_blocks * BLOCK - q_total
    query_pos = first_query + jnp.arange(q_total, dtype=jnp.int32)

    def visit_block(turn_index, state_carry, block_order):
        run_peak, run_total, run_out = state_carry
        local_block = block_order[turn_index]
        key_block = lax.dynamic_slice_in_dim(cache_keys, local_block * BLOCK, BLOCK, 0)
        value_block = lax.dynamic_slice_in_dim(cache_values, local_block * BLOCK, BLOCK, 0)
        picked = lax.dynamic_index_in_dim(chosen, local_block, 2, keepdims=False)
        picked_rows = jnp.repeat(picked, BLOCK, axis=0)
        key_pos = ctx_place * local_len + local_block * BLOCK + jnp.arange(BLOCK, dtype=jnp.int32)
        allowed_mask = picked_rows[:, :, None] & (
            key_pos[None, None, :] <= query_pos[:, None, None]
        )
        block_peak, block_total, block_out = block_terms(
            q_four, key_block, value_block, allowed_mask, score_scale
        )
        new_peak = jnp.maximum(run_peak, block_peak)
        old_factor = jnp.exp(run_peak - new_peak)
        new_factor = jnp.exp(block_peak - new_peak)
        new_total = run_total * old_factor + block_total * new_factor
        new_out = run_out * old_factor[..., None] + block_out * new_factor[..., None]
        return (new_peak, new_total, new_out)

    start_carry = (
        jnp.full((q_total, heads_local), NEG_FILL, jnp.float32),
        jnp.zeros((q_total, heads_local), jnp.float32),
        jnp.zeros((q_total, heads_local, head_width), jnp.float32),
    )
    block_order = jnp.arange(local_blocks, dtype=jnp.int32)
    local_peak, local_total, local_out = lax.fori_loop(
        0, local_blocks, partial(visit_block, block_order=block_order), start_carry
    )
    top_peak = lax.pmax(local_peak, "ctx")
    factor = jnp.exp(local_peak - top_peak)
    out_sum, total_sum = lax.psum((local_out * factor[..., None], local_total * factor), "ctx")
    attention = (
        (out_sum / total_sum[..., None])
        .reshape(q_total, heads_local * head_width)
        .astype(jnp.bfloat16)
    )
    return lax.psum_scatter(
        jnp.dot(attention, out_weight, preferred_element_type=jnp.float32),
        "head",
        scatter_dimension=0,
        tiled=True,
    ).astype(jnp.bfloat16)


def solution(mesh):
    return jax.shard_map(
        body,
        mesh=mesh,
        in_specs=(
            P("ctx", "head"),
            P("ctx", "head", None),
            P("ctx", "head", None),
            P("head", None),
            P("head", None),
            P("head", "ctx"),
        ),
        out_specs=P("head", "ctx"),
        check_vma=False,
    )
```

profile of v0, /device:TPU:8, one launch (start us, length us, event | category | flops | bytes accessed | tf_op | source)
XLA Modules:
  0.0 755.4 jit_solution(7034202437298603779)
XLA Ops:
  6.5 0.7 all-gather.2.cloned.1.call-update
  7.4 0.8 compare_reduce_fusion.1
  8.2 1.4 compare_reduce_fusion
  9.7 86.6 %all-gather.2.cloned.1.call-done = bf16[512,1024]{1,0:T(8,128)(2,1)} async-done(((bf16[8,1024]{1,0:T(8,128)(2,1)}), bf16[512,1024]{1,0:T(8,128)(2,1)}) %all-gather.2.cloned.1.call-update) | async-done | bytes 1048592 | tf_op jit(solution)/shard_map/all_gather | solution.py:40
  96.3 2.3 copy.18
  98.6 1.6 copy.20
  100.3 60.9 %while.20 = (s32[]{:T(128)}, f32[512,8]{0,1:T(8,128)S(1)}, f32[512,8]{0,1:T(8,128)S(1)}, f32[512,8,128]{0,2,1:T(8,128)S(1)}, s32[8]{0:T(128)S(1)}, /*index=5*/pr...) while((s32[]{:T(128)}, f32[512,8]{0,1:T(8,128)S(1)}, ...), condition=%wide.region_5.6_spmd.clone, body=%wide.region_2.5_spmd.clone.sunk | while | flops 279020160 | bytes 12146040 | solution.py:86
  100.3 0.7 dynamic_slice.59
  103.8 0.1 broadcast_compare_fusion.2
  103.9 1.3 fusion.38
  105.3 0.6 convert_reduce_fusion.2
  105.9 1.9 fusion.40
  107.9 0.7 dynamic_slice.59
  111.4 0.1 broadcast_compare_fusion.2
  111.5 1.3 fusion.38
  112.9 0.6 convert_reduce_fusion.2
  113.5 1.9 fusion.40
  115.5 0.7 dynamic_slice.59
  119.2 1.3 fusion.38
  120.5 0.6 convert_reduce_fusion.2
  121.1 1.9 fusion.40
  123.1 0.7 dynamic_slice.59
  126.8 1.3 fusion.38
  128.1 0.6 convert_reduce_fusion.2
  128.8 1.9 fusion.40
  130.7 0.7 dynamic_slice.59
  134.4 1.3 fusion.38
  135.7 0.6 convert_reduce_fusion.2
  136.4 1.9 fusion.40
  138.3 0.7 dynamic_slice.59
  142.0 1.3 fusion.38
  143.4 0.6 convert_reduce_fusion.2
  144.0 1.9 fusion.40
  145.9 0.7 dynamic_slice.59
  149.6 1.3 fusion.38
  151.0 0.6 convert_reduce_fusion.2
  151.6 1.9 fusion.40
  153.6 0.7 dynamic_slice.59
  157.2 1.3 fusion.38
  158.6 0.6 convert_reduce_fusion.2
  159.2 1.9 fusion.40
  161.2 272.2 %pmax.7 = f32[512,8]{0,1:T(8,128)S(1)} all-reduce(f32[512,8]{0,1:T(8,128)S(1)} %get-tuple-element.262), channel_id=1, replica_groups=mesh['ctx'=64,'head'=8] {'ctx'}, use_global_device_ids=true, to_apply=%region_6.7 | all-reduce | flops 4096 | bytes 32768 | tf_op jit(solution)/shard_map/pmax | solution.py:89
  433.4 1.6 broadcast_multiply_fusion
  435.1 276.5 %psum.15 = f32[512,8]{0,1:T(8,128)S(1)} all-reduce(f32[512,8]{0,1:T(8,128)S(1)} %get-tuple-element.363), channel_id=1, replica_groups=mesh['ctx'=64,'head'=8] {'ctx'}, use_global_device_ids=true, to_apply=%region_8.9 | all-reduce | flops 4096 | bytes 32768 | tf_op jit(solution)/shard_map/psum | solution.py:91
  711.6 1.9 divide_convert_fusion
  713.5 1.2 fusion.28
  714.7 32.8 %reduce-scatter.2.cloned.1.call-done = f32[64,128]{1,0:T(8,128)} async-done(((f32[512,128]{1,0:T(8,128)}), f32[64,128]{1,0:T(8,128)}) %reduce-scatter.2.cloned.1.call-update) | async-done | bytes 32784 | tf_op jit(solution)/shard_map/reduce_scatter | solution.py:97
  747.5 1.4 convert_element_type.36
  (72 shorter events, 1.9 us)
Async XLA Ops:
  6.5 706.9 %copy-start = (bf16[1024,128]{1,0:T(8,128)(2,1)S(1)}, bf16[1024,128]{1,0:T(8,128)(2,1)}, u32[]{:S(2)}) copy-start(bf16[1024,128]{1,0:T(8,128)(2,1)} %param.13) | copy-start | bytes 786436
  6.5 89.8 %all-gather.2.cloned.1.call-start = ((), (), s32[]{:S(2)}) async-start(), calls=%async_computation.1 | async-start | bytes 1064960 | tf_op jit(solution)/shard_map/all_gather | solution.py:40
  7.3 704.3 %all-reduce.2.cloned.1.call-start = ((), (), s32[]{:S(2)}) async-start(), calls=%async_computation.2 | async-start | bytes 4194304 | tf_op jit(solution)/shard_map/psum | solution.py:91
  435.1 312.4 %reduce-scatter.2.cloned.1.call-start = ((), (), s32[]{:S(2)}) async-start(), calls=%async_computation.3 | async-start | bytes 294912 | tf_op jit(solution)/shard_map/reduce_scatter | solution.py:97
Sparse Core Ops, SparseCore 0:
  10.4 85.8 all-gather.1
  435.2 162.4 all-reduce.1
  714.8 32.6 reduce-scatter.1
where the time goes:
time: 757 us; the launch traced here: 755 us
  blocking collectives  549 us (73%)
  waiting for transfers between devices  120 us (16%)
  matrix products  27.4 us (4%)
  loops' own time  22.9 us (3%)
  between operations  13.2 us (2%)
  other arithmetic  12.9 us (2%)
  local copies, waits for them, and re-layouts  10 us (1%)
    psum x1, blocking collectives, body(): lax.psum((local_out * factor[..., None], local_total * factor), 'ctx')  276 us
    pmax x1, blocking collectives, body(): top_peak = lax.pmax(local_peak, 'ctx')  272 us
    all_gather x1, waiting for transfers between devices, body(): q_whole = lax.all_gather(queries, 'ctx', axis=0, tiled=True)  86.6 us
    reduce_scatter x1, waiting for transfers between devices, body(): lax.psum_scatter(jnp.dot(attention, out_weight, preferred_element_type=jn...  32.8 us
    another operation x1, loops' own time, body(): lax.fori_loop(0, local_blocks, partial(visit_block, block_order=block_ord...  22.9 us
    dot_general x8, matrix products, block_terms(): jnp.einsum('qgjk,kgd->qgjd', weights_four, value_block, preferred_element...  15.5 us
  transfers between devices with their start and end apart: 3, of which 2 were waited for; matrix products, arithmetic and copies ran while one was open for 0% of the time, Pallas kernels for 0%

commit v1 on v0

--- a/solution.py
+++ b/solution.py
@@ -6,6 +6,13 @@
 
 BLOCK = 128
 NEG_FILL = -1e30
+
+
+def swapped_in(x, axis, dim):
+    size = lax.axis_size(axis)
+    blocks = jnp.stack([x for _ in range(size)])
+    blocks = lax.all_to_all(blocks, axis, split_axis=0, concat_axis=0)
+    return jnp.concatenate(blocks, axis=dim)
 
 
 def block_terms(q_four, key_block, value_block, allowed_mask, score_scale):
@@ -37,7 +44,7 @@
 def body(queries, cache_keys, cache_values, vertical_blocks, slash_offsets, out_weight):
     ctx_count = lax.axis_size("ctx")
     ctx_place = lax.axis_index("ctx")
-    q_whole = lax.all_gather(queries, "ctx", axis=0, tiled=True)
+    q_whole = swapped_in(queries, "ctx", 0)
     q_total = q_whole.shape[0]
     local_len, kv_local, head_width = cache_keys.shape
     heads_local = vertical_blocks.shape[0]

time: 757 us -> 710 us (0.938)
  waiting for transfers between devices: 120 us -> 59.6 us
  starting transfers between devices: 0.08 us -> 16.7 us
    all_gather x1 -> x0, waiting for transfers between devices: 86.6 us -> none  [body(): q_whole = lax.all_gather(queries, 'ctx', axis=0, tiled=True)]
    all_to_all x0 -> x1, waiting for transfers between devices: none -> 28.1 us  [swapped_in(): blocks = lax.all_to_all(blocks, axis, split_axis=0, concat_axis=0)]
    all_to_all x0 -> x1, starting transfers between devices: none -> 16.6 us  [swapped_in(): blocks = lax.all_to_all(blocks, axis, split_axis=0, concat_axis=0)]
where the time goes in v1:
time: 710 us; the launch traced here: 709 us
  blocking collectives  549 us (77%)
  waiting for transfers between devices  59.6 us (8%)
  matrix products  27.4 us (4%)
  loops' own time  22.9 us (3%)
  starting transfers between devices  16.7 us (2%)
  between operations  13.5 us (2%)
  other arithmetic  11.6 us (2%)
  local copies, waits for them, and re-layouts  8.39 us (1%)
    psum x1, blocking collectives, body(): lax.psum((local_out * factor[..., None], local_total * factor), 'ctx')  277 us
    pmax x1, blocking collectives, body(): top_peak = lax.pmax(local_peak, 'ctx')  272 us
    reduce_scatter x1, waiting for transfers between devices, body(): lax.psum_scatter(jnp.dot(attention, out_weight, preferred_element_type=jn...  31.4 us
    all_to_all x1, waiting for transfers between devices, swapped_in(): blocks = lax.all_to_all(blocks, axis, split_axis=0, concat_axis=0)  28.1 us
    another operation x1, loops' own time, body(): lax.fori_loop(0, local_blocks, partial(visit_block, block_order=block_ord...  22.9 us
    all_to_all x1, starting transfers between devices, swapped_in(): blocks = lax.all_to_all(blocks, axis, split_axis=0, concat_axis=0)  16.6 us
    dot_general x8, matrix products, block_terms(): jnp.einsum('qgjk,kgd->qgjd', weights_four, value_block, preferred_element...  15.5 us
  transfers between devices with their start and end apart: 3, of which 2 were waited for; matrix products, arithmetic and copies ran while one was open for 0% of the time, Pallas kernels for 0%

profile of v1, /device:TPU:8, one launch (start us, length us, event | category | flops | bytes accessed | tf_op | source)
XLA Modules:
  0.0 708.8 jit_solution(7103123090716757143)
XLA Ops:
  6.5 1.9 stack.2
  8.4 16.6 %all-to-all-start = ((bf16[64,8,1024]{2,1,0:T(8,128)(2,1)}), bf16[64,8,1024]{2,1,0:T(8,128)(2,1)S(1)}, u32[]{:S(2)}, u32[]{:S(2)}) async-start(bf16[64,8,1024]{2,1,0:T(8,128)(2,1)} %stack.2), calls=%async_computation | async-start | bytes 2097152 | tf_op jit(solution)/shard_map/all_to_all | solution.py:14
  25.3 0.7 compare_reduce_fusion
  26.1 28.1 %all-to-all-done = bf16[64,8,1024]{2,1,0:T(8,128)(2,1)S(1)} async-done(((bf16[64,8,1024]{2,1,0:T(8,128)(2,1)}), bf16[64,8,1024]{2,1,0:T(8,128)(2,1)S(1)}, u32[]{:S(2)}, u32[]{:S(2)}) %all-to-all-start) | async-done | bytes 1048608 | tf_op jit(solution)/shard_map/all_to_all | solution.py:14
  54.3 0.3 copy.18
  54.5 0.1 copy.14
  54.7 60.9 %while.20 = (s32[]{:T(128)}, f32[512,8]{0,1:T(8,128)S(1)}, f32[512,8]{0,1:T(8,128)S(1)}, f32[512,8,128]{0,2,1:T(8,128)S(1)}, s32[8]{0:T(128)S(1)}, /*index=5*/pr...) while((s32[]{:T(128)}, f32[512,8]{0,1:T(8,128)S(1)}, ...), condition=%wide.region_5.6_spmd.clone, body=%wide.region_2.5_spmd.clone.sunk | while | flops 279020160 | bytes 12146040 | solution.py:93
  54.7 0.7 dynamic_slice.59
  58.4 1.3 fusion.38
  59.7 0.6 convert_reduce_fusion.2
  60.4 1.9 fusion.40
  62.3 0.7 dynamic_slice.59
  66.0 1.3 fusion.38
  67.3 0.6 convert_reduce_fusion.2
  68.0 1.9 fusion.40
  69.9 0.7 dynamic_slice.59
  73.5 0.1 broadcast_compare_fusion.2
  73.6 1.3 fusion.38
  75.0 0.6 convert_reduce_fusion.2
  75.6 1.9 fusion.40
  77.5 0.7 dynamic_slice.59
  81.2 1.3 fusion.38
  82.6 0.6 convert_reduce_fusion.2
  83.2 1.9 fusion.40
  85.2 0.7 dynamic_slice.59
  88.7 0.1 broadcast_compare_fusion.2
  88.8 1.3 fusion.38
  90.2 0.6 convert_reduce_fusion.2
  90.8 1.9 fusion.40
  92.8 0.7 dynamic_slice.59
  96.4 1.3 fusion.38
  97.8 0.6 convert_reduce_fusion.2
  98.4 1.9 fusion.40
  100.4 0.7 dynamic_slice.59
  104.0 1.3 fusion.38
  105.4 0.6 convert_reduce_fusion.2
  106.0 1.9 fusion.40
  108.0 0.7 dynamic_slice.59
  111.7 1.3 fusion.38
  113.0 0.6 convert_reduce_fusion.2
  113.6 1.9 fusion.40
  115.6 271.9 %pmax.7 = f32[512,8]{0,1:T(8,128)S(1)} all-reduce(f32[512,8]{0,1:T(8,128)S(1)} %get-tuple-element.262), channel_id=1, replica_groups=mesh['ctx'=64,'head'=8] {'ctx'}, use_global_device_ids=true, to_apply=%region_6.7 | all-reduce | flops 4096 | bytes 32768 | tf_op jit(solution)/shard_map/pmax | solution.py:96
  387.5 1.6 broadcast_multiply_fusion
  389.2 276.8 %psum.15 = f32[512,8]{0,1:T(8,128)S(1)} all-reduce(f32[512,8]{0,1:T(8,128)S(1)} %get-tuple-element.353), channel_id=1, replica_groups=mesh['ctx'=64,'head'=8] {'ctx'}, use_global_device_ids=true, to_apply=%region_8.9 | all-reduce | flops 4096 | bytes 32768 | tf_op jit(solution)/shard_map/psum | solution.py:98
  666.1 1.9 divide_convert_fusion
  667.9 1.2 fusion.28
  669.1 31.4 %reduce-scatter.2.cloned.1.call-done = f32[64,128]{1,0:T(8,128)} async-done(((f32[512,128]{1,0:T(8,128)}), f32[64,128]{1,0:T(8,128)}) %reduce-scatter.2.cloned.1.call-update) | async-done | bytes 32784 | tf_op jit(solution)/shard_map/reduce_scatter | solution.py:104
  700.6 1.4 convert_element_type.36
  (76 shorter events, 2.0 us)
Async XLA Ops:
  6.5 661.4 %copy-start = (bf16[1024,128]{1,0:T(8,128)(2,1)S(1)}, bf16[1024,128]{1,0:T(8,128)(2,1)}, u32[]{:S(2)}) copy-start(bf16[1024,128]{1,0:T(8,128)(2,1)} %param.13) | copy-start | bytes 786436
  6.5 18.6 %copy-start.1 = (s32[8,8]{1,0:T(8,128)S(1)}, s32[8,8]{1,0:T(8,128)}, u32[]{:S(2)}) copy-start(s32[8,8]{1,0:T(8,128)} %param.11) | copy-start | bytes 772
  6.5 18.8 %copy-start.2 = (s32[8,48]{1,0:T(8,128)S(1)}, s32[8,48]{1,0:T(8,128)}, u32[]{:S(2)}) copy-start(s32[8,48]{1,0:T(8,128)} %param.12) | copy-start | bytes 4612
  8.4 45.8 %all-to-all-start = ((bf16[64,8,1024]{2,1,0:T(8,128)(2,1)}), bf16[64,8,1024]{2,1,0:T(8,128)(2,1)S(1)}, u32[]{:S(2)}, u32[]{:S(2)}) async-start(bf16[64,8,1024]{2,1,0:T(8,128)(2,1)} %stack.2), calls=%async_computation | async-start | bytes 2097152 | tf_op jit(solution)/shard_map/all_to_all | solution.py:14
  25.0 641.0 %all-reduce.2.cloned.1.call-start = ((), (), s32[]{:S(2)}) async-start(), calls=%async_computation.2 | async-start | bytes 4194304 | tf_op jit(solution)/shard_map/psum | solution.py:98
  389.2 311.4 %reduce-scatter.2.cloned.1.call-start = ((), (), s32[]{:S(2)}) async-start(), calls=%async_computation.3 | async-start | bytes 294912 | tf_op jit(solution)/shard_map/reduce_scatter | solution.py:104
Sparse Core Ops, SparseCore 0:
  389.3 160.9 all-reduce.1
  669.3 31.2 reduce-scatter.1
